TPU v7x, 32 devices: a whole 2x2x4 slice. The times are simulated.
32 devices in a mesh: groups: 2 (over y), ex: 4 (over z), layer: 4 (over x, core).
Axes of the slice: x: 2, y: 2, z: 4, core: 2. Of those that a mesh axis runs over, the one named last changes fastest.
Arguments:
- queries: bfloat16 [256, 16384], P('ex', 'layer'), may hold values from -6 to 6
- train_grads: bfloat16 [3072, 16384], P(('groups', 'ex'), 'layer'), parts along dimension 0, may hold values from -1800 to 1800
- layer_start: int32 [32], replicated, may hold values from 0 to 16128, as said below
Outputs:
- scores: float32 [3072, 256], P(('groups', 'ex', 'layer')), parts along dimension 0
There are 2 independent parts, one for each index of `groups`. A program takes and returns all parts, laid end to end along the dimension named above; an argument that names none is the same for every part. Nothing has to cross between parts.
Inputs may be any that keep to these rules, and one draw needn't show every extreme that they name: layer_start[0] is 0 and it rises; each layer has 256 to 3 * (256) columns, both bounds reached, and the layers end at 16384.
All inputs are finite; a program needn't handle non-finite values.
Results may differ from a plain program's by a relative error of at most 0.0029.
Values may be sent and summed in bfloat16 or wider, within the bound.
A program may use at most 64 MiB of HBM per device.

v0:
```python
import jax
import jax.numpy as jnp
from jax import lax
from jax.sharding import PartitionSpec as P

WIDTH = 16384


EPSILON = 1e-05


def body(queries, train_grads, layer_start):
    width_dev = train_grads.shape[1]
    offset_cols = lax.axis_index("layer") * width_dev
    layer_end = jnp.concatenate([layer_start[1:], jnp.array([WIDTH], jnp.int32)])
    columns = offset_cols + jnp.arange(width_dev, dtype=jnp.int32)
    member = (
        (columns[:, None] >= layer_start[None, :]) & (columns[:, None] < layer_end[None, :])
    ).astype(jnp.float32)
    counts = (layer_end - layer_start).astype(jnp.float32)
    widened = train_grads.astype(jnp.float32)
    local_sums = jnp.dot(widened * widened, member, precision=lax.Precision.HIGHEST)
    square_sums = lax.psum(local_sums, "layer")
    overall = jnp.sum(square_sums, axis=1, keepdims=True) / WIDTH
    inv_norm = lax.rsqrt(square_sums / counts + overall + EPSILON) * WIDTH ** (-0.5)
    col_scale = jnp.dot(inv_norm, member.T, precision=lax.Precision.HIGHEST)
    scaled = (widened * col_scale).astype(jnp.bfloat16)
    every_q = lax.all_gather(queries, "ex", axis=0, tiled=True)
    partial_value = lax.dot_general(
        scaled, every_q, (((1,), (1,)), ((), ())), preferred_element_type=jnp.float32
    )
    return lax.psum_scatter(partial_value, "layer", scatter_dimension=0, tiled=True)


def solution(mesh):
    in_specs = (P("ex", "layer"), P(("groups", "ex"), "layer"), P())
    out_specs = P(("groups", "ex", "layer"), None)
    return jax.shard_map(body, mesh=mesh, in_specs=in_specs, out_specs=out_specs, check_vma=False)
```

profile of v0, /device:TPU:0, one launch (start us, length us, event | category | flops | bytes accessed | tf_op | source)
XLA Modules:
  0.0 88.5 jit_solution(10686614074799115491)
XLA Ops:
  6.5 0.0 copy-start.1
  6.5 0.0 copy-start
  6.5 0.0 all-gather.2.cloned.1.call-start
  6.5 0.7 all-gather.2.cloned.1.call-update
  7.3 0.0 reduce-scatter.2.cloned.1.call-start
  7.3 0.9 %slice.3 = s32[31]{0:T(128)S(1)} slice(s32[32]{0:T(128)} %param.6), slice={[1:32]} | slice | bytes 248 | tf_op jit(solution)/shard_map/slice | solution.py:15
  8.2 0.7 subtract_convert_fusion
  9.0 5.4 %fusion = f32[384,32]{0,1:T(8,128)S(1)} fusion(bf16[384,4096]{1,0:T(8,128)(2,1)} %param.5, s32[4096]{0:T(1024)S(1)} %iota_add_fusion, s32[32]{0:T(128)S(1)} %get-tuple-element.6, s32[32]{0:T(128)} %param.6), kind=kOutput, calls=%fused_computation.2 | convolution fusion | flops 607518720 | bytes 3211520 | tf_op jit(solution)/shard_map/dot_general | solution.py:22
  14.4 13.6 %psum.7 = f32[384,32]{0,1:T(8,128)S(1)} all-reduce(f32[384,32]{0,1:T(8,128)S(1)} %fusion), channel_id=1, replica_groups=mesh['groups'=2,'ex'=4,'layer'=4] {'layer'}, use_global_device_ids=true, to_apply=%region_0.0 | all-reduce | flops 12288 | bytes 98304 | tf_op jit(solution)/shard_map/psum | solution.py:23
  28.0 0.0 copy-done.1
  28.1 0.0 copy-done
  28.1 4.6 %fusion.1 = bf16[384,4096]{1,0:T(8,128)(2,1)} fusion(bf16[384,4096]{1,0:T(8,128)(2,1)S(1)} %copy-done, s32[4096]{0:T(1024)S(1)} %iota_add_fusion, s32[32]{0:T(128)S(1)} %get-tuple-element.6, s32[32]{0:T(128)S(1)} %copy-done.1, f32[384,32]{0,1:T(8,128)S(1)} %psum.7, f32[384]{0:T(512)S(1)} %broadcast_multiply_fusion, f32[32]{0:T(128)S(1)} %get-tuple-element.5), kind=kOutput, calls=%fused_computation.3 | convolution fusion | flops 609140736 | bytes 6358912 | tf_op jit(solution)/shard_map/dot_general | solution.py:26
  32.6 25.0 %all-gather.2.cloned.1.call-done = bf16[256,4096]{1,0:T(8,128)(2,1)} async-done(((bf16[64,4096]{1,0:T(8,128)(2,1)}), bf16[256,4096]{1,0:T(8,128)(2,1)}) %all-gather.2.cloned.1.call-update) | async-done | bytes 2097168 | tf_op jit(solution)/shard_map/all_gather | solution.py:28
  57.6 4.3 %fusion.19 = f32[384,256]{1,0:T(8,128)} fusion(bf16[384,4096]{1,0:T(8,128)(2,1)} %fusion.1, bf16[256,4096]{1,0:T(8,128)(2,1)} %all-gather.2.cloned.1.call-done), kind=kOutput, calls=%fused_computation.26 | convolution fusion | flops 805306368 | bytes 5636096 | tf_op jit(solution)/shard_map/dot_general | solution.py:29
  61.9 0.0 reduce-scatter.2.cloned.1.call-update
  61.9 19.7 %reduce-scatter.2.cloned.1.call-done = f32[96,256]{1,0:T(8,128)} async-done(((f32[384,256]{1,0:T(8,128)}), f32[96,256]{1,0:T(8,128)}) %reduce-scatter.2.cloned.1.call-update) | async-done | bytes 98320 | tf_op jit(solution)/shard_map/reduce_scatter | solution.py:32
  (3 shorter events, 0.0 us)
Async XLA Ops:
  6.5 21.5 %copy-start.1 = (s32[32]{0:T(128)S(1)}, s32[32]{0:T(128)}, u32[]{:S(2)}) copy-start(s32[32]{0:T(128)} %param.6) | copy-start | bytes 388
  6.5 21.5 %copy-start = (bf16[384,4096]{1,0:T(8,128)(2,1)S(1)}, bf16[384,4096]{1,0:T(8,128)(2,1)}, u32[]{:S(2)}) copy-start(bf16[384,4096]{1,0:T(8,128)(2,1)} %param.5) | copy-start | bytes 9437188
  6.5 51.1 %all-gather.2.cloned.1.call-start = ((), (), s32[]{:S(2)}) async-start(), calls=%async_computation.1 | async-start | bytes 2621440 | tf_op jit(solution)/shard_map/all_gather | solution.py:28
  7.3 74.4 %reduce-scatter.2.cloned.1.call-start = ((), (), s32[]{:S(2)}) async-start(), calls=%async_computation.2 | async-start | bytes 491520 | tf_op jit(solution)/shard_map/reduce_scatter | solution.py:32
Sparse Core Ops, SparseCore 0:
  8.9 48.6 all-gather.1
  62.1 19.5 reduce-scatter.1
where the time goes:
time: 88.7 us; the launch traced here: 88.5 us
  waiting for transfers between devices  45.4 us (51%)
  matrix products  14.3 us (16%)
  blocking collectives  13.6 us (15%)
  between operations  13.4 us (15%)
  local copies, waits for them, and re-layouts  0.92 us (1%)
    all_gather x1, waiting for transfers between devices, body(): every_q = lax.all_gather(queries, 'ex', axis=0, tiled=True)  25 us
    reduce_scatter x1, waiting for transfers between devices, body(): lax.psum_scatter(partial_value, 'layer', scatter_dimension=0, tiled=True)  19.7 us
    psum x1, blocking collectives, body(): square_sums = lax.psum(local_sums, 'layer')  13.6 us
    dot_general x1, matrix products, body(): jnp.dot(widened * widened, member, precision=lax.Precision.HIGHEST)  5.42 us
    dot_general x1, matrix products, body(): col_scale = jnp.dot(inv_norm, member.T, precision=lax.Precision.HIGHEST)  4.55 us
    dot_general x1, matrix products, body(): lax.dot_general(scaled, every_q, (((1,), (1,)), ((), ())), preferred_elem...  4.32 us
  transfers between devices with their start and end apart: 2, of which 2 were waited for; matrix products, arithmetic and copies ran while one was open for 13% of the time, Pallas kernels for 0%

commit v1 on v0

v1 whole, which is shorter than its diff:
```python
import functools

import jax
import jax.numpy as jnp
from jax import lax
from jax.experimental import pallas as pl
from jax.experimental.pallas import tpu as pltpu
from jax.sharding import PartitionSpec as P

WIDTH = 16384
EPSILON = 1e-05
MESH = pl.DeviceIdType.MESH
LANES = 128


def nt_dot(a, b):
    return lax.dot_general(a, b, (((1,), (1,)), ((), ())), preferred_element_type=jnp.float32)


def kernel(
    n, groups, parts, chunks, start_ref, q_ref, x_hbm, out_ref,
    x_v, scaled_v, q_all, sums, sums_in, inv_v, acc, acc_in,
    x_sem, q_sem, z_send, z_recv, y_send, y_recv, sum_send, sum_recv, acc_send, acc_recv,
):
    y, z, me = lax.axis_index("groups"), lax.axis_index("ex"), lax.axis_index("layer")
    rows, width = q_ref.shape
    share = rows // groups
    chunk = width // chunks
    examples = x_hbm.shape[0]
    kept = examples // parts
    layers = start_ref.shape[0]
    last = n - 2
    pairs = n // 2

    def cols(c):
        return pl.ds(c * chunk, chunk)

    def x_copy(c):
        return pltpu.make_async_copy(x_hbm.at[:, cols(c)], x_v.at[:, cols(c)], x_sem.at[c])

    def block_rows(b):
        return pl.ds(pl.multiple_of(b * rows, rows), rows)

    def share_rows(b, g):
        return pl.ds(pl.multiple_of(b * rows + g * share, share), share)

    def z_target(flow):
        return z + 1 if flow == 0 else z - 1

    def has_target(flow):
        return z + 1 < n if flow == 0 else z > 0

    def arriving(flow, s):
        return z - 1 - s if flow == 0 else z + 1 + s

    def arrives(flow, s):
        return z - 1 - s >= 0 if flow == 0 else z + 1 + s < n

    def z_copy(flow, s, c, b, own=False):
        there = q_all.at[share_rows(b, y), cols(c)]
        here = q_ref.at[pl.ds(pl.multiple_of(y * share, share), share), cols(c)] if own else there
        return pltpu.make_async_remote_copy(
            src_ref=here, dst_ref=there, send_sem=z_send.at[flow, s, c], recv_sem=z_recv.at[flow, s, c],
            device_id={"ex": z_target(flow)}, device_id_type=MESH)

    def y_copy(flow, s, g, c, b, owner):
        block = q_all.at[share_rows(b, owner), cols(c)]
        return pltpu.make_async_remote_copy(
            src_ref=block, dst_ref=block, send_sem=y_send.at[flow, s, g - 1, c], recv_sem=y_recv.at[flow, s, g - 1, c],
            device_id={"groups": lax.rem(y + g, groups)}, device_id_type=MESH)

    def sum_copy(r):
        return pltpu.make_async_remote_copy(
            src_ref=sums, dst_ref=sums_in.at[r - 1], send_sem=sum_send.at[r - 1], recv_sem=sum_recv.at[r - 1],
            device_id={"layer": lax.rem(me + r, parts)}, device_id_type=MESH)

    def acc_copy(k, r):
        to = lax.rem(me + r, parts)
        return pltpu.make_async_remote_copy(
            src_ref=acc.at[k, pl.ds(pl.multiple_of(to * kept, 8), kept)], dst_ref=acc_in.at[k, r - 1],
            send_sem=acc_send.at[k, r - 1], recv_sem=acc_recv.at[k, r - 1],
            device_id={"layer": to}, device_id_type=MESH)

    def handle(s, c):
        for flow in (1, 0):
            @pl.when(arrives(flow, s))
            def _():
                b = arriving(flow, s)
                z_copy(flow, s, c, b).wait_recv()
                for g in range(1, groups):
                    y_copy(flow, s, g, c, b, y).start()
                if s < last:
                    @pl.when(has_target(flow))
                    def _():
                        z_copy(flow, s + 1, c, b).start()

    def wait_y(s, c):
        for flow in (1, 0):
            @pl.when(arrives(flow, s))
            def _():
                b = arriving(flow, s)
                for g in range(1, groups):
                    y_copy(flow, s, g, c, b, lax.rem(y + groups - g, groups)).wait_recv()

    for c in range(chunks):
        x_copy(c).start()
    q_copy = pltpu.make_async_copy(q_ref, q_all.at[block_rows(z)], q_sem)
    q_copy.start()

    barrier = pltpu.get_barrier_semaphore()
    for flow in (0, 1):
        @pl.when(has_target(flow))
        def _():
            pl.semaphore_signal(barrier, inc=1, device_id={"ex": z_target(flow)}, device_id_type=MESH)
    for g in range(1, groups):
        pl.semaphore_signal(barrier, inc=1, device_id={"groups": lax.rem(y + g, groups)}, device_id_type=MESH)
    for r in range(1, parts):
        pl.semaphore_signal(barrier, inc=1, device_id={"layer": lax.rem(me + r, parts)}, device_id_type=MESH)
    peers = groups + parts - jnp.where(z == 0, 1, 0) - jnp.where(z == n - 1, 1, 0)
    pl.semaphore_wait(barrier, peers)

    for c in range(chunks):
        for flow in (1, 0):
            @pl.when(has_target(flow))
            def _():
                z_copy(flow, 0, c, z, own=True).start()

    starts = [start_ref[l] for l in range(layers)]
    ends = starts[1:] + [WIDTH]
    offset = me * width

    def table(index):
        low = jnp.full(index.shape, WIDTH, jnp.int32)
        high = jnp.full(index.shape, 0, jnp.int32)
        for l in range(layers):
            low = jnp.where(index == l, starts[l], low)
            high = jnp.where(index == l, ends[l], high)
        return low - offset, high - offset

    lane_low, lane_high = table(lax.broadcasted_iota(jnp.int32, (1, LANES), 1))
    sub = lax.broadcasted_iota(jnp.int32, (LANES, 1), 0)
    pieces = 3
    sub_low, sub_high = table(jnp.where(sub < pieces * layers, lax.rem(sub, layers), layers))

    total = jnp.zeros((examples, LANES), jnp.float32)
    for c in range(chunks):
        x_copy(c).wait()
        column = c * chunk + lax.broadcasted_iota(jnp.int32, (chunk, LANES), 0)
        member = ((column >= lane_low) & (column < lane_high)).astype(jnp.float32).astype(jnp.bfloat16)
        wide = x_v[:, cols(c)].astype(jnp.float32)
        square = wide * wide
        big = square.astype(jnp.bfloat16)
        small = (square - big.astype(jnp.float32)).astype(jnp.bfloat16)
        total += jnp.dot(big, member, preferred_element_type=jnp.float32)
        total += jnp.dot(small, member, preferred_element_type=jnp.float32)
        handle(0, c)
    sums[...] = total.T[:layers]
    for r in range(1, parts):
        sum_copy(r).start()

    q_copy.wait()
    own_pair = z // 2

    def pair_dot(k, p, c):
        pair = pl.ds(pl.multiple_of(p * 2 * rows, 2 * rows), 2 * rows)
        value = nt_dot(scaled_v[:, cols(c)], q_all[pair, cols(c)])
        if c == 0:
            acc[k] = value
        else:
            acc[k] += value

    def send_pair(k):
        for r in range(1, parts):
            acc_copy(k, r).start()

    for c in range(chunks):
        if last >= 1:
            handle(1, c)
        if c == 0:
            for r in range(1, parts):
                sum_copy(r).wait_recv()
            tot = sums[...]
            for r in range(1, parts):
                tot += sums_in[r - 1]
            low, high = sub_low[:layers], sub_high[:layers]
            counts = (high - low).astype(jnp.float32)
            overall = jnp.sum(tot, axis=0, keepdims=True) / WIDTH
            inv = lax.rsqrt(tot / counts + overall + EPSILON) * WIDTH ** (-0.5)
            split = []
            rest = inv
            for _ in range(pieces):
                piece = rest.astype(jnp.bfloat16).astype(jnp.float32)
                split.append(piece)
                rest = rest - piece
            split.append(jnp.zeros((LANES - pieces * layers, examples), jnp.float32))
            inv_v[...] = jnp.concatenate(split, axis=0).T.astype(jnp.bfloat16)
        column = c * chunk + lax.broadcasted_iota(jnp.int32, (LANES, chunk), 1)
        member = ((column >= sub_low) & (column < sub_high)).astype(jnp.float32).astype(jnp.bfloat16)
        scale = jnp.dot(inv_v[...], member, preferred_element_type=jnp.float32)
        scaled_v[:, cols(c)] = (x_v[:, cols(c)].astype(jnp.float32) * scale).astype(jnp.bfloat16)
        wait_y(0, c)
        pair_dot(0, own_pair, c)
    send_pair(0)

    ahead = z < n // 2
    last_pair = jnp.where(ahead, pairs - 1, 0)
    pair_of = [own_pair]
    for s in range(2, last):
        for c in range(chunks):
            handle(s, c)
    handle(last, 0)
    for s in range(1, last):
        for c in range(chunks):
            wait_y(s, c)
    for k in range(1, pairs - 1):
        p = jnp.where(ahead, k - 1, k)
        p = p + jnp.where(p >= own_pair, 1, 0)
        pair_of.append(p)
        for c in range(chunks):
            pair_dot(k, p, c)
        send_pair(k)
    pair_of.append(last_pair)
    for c in range(chunks):
        if c + 1 < chunks:
            handle(last, c + 1)
        wait_y(last, c)
        pair_dot(pairs - 1, last_pair, c)
    send_pair(pairs - 1)

    mine = pl.ds(pl.multiple_of(me * kept, 8), kept)
    for k in range(pairs):
        value = acc[k, mine]
        for r in range(1, parts):
            acc_copy(k, r).wait_recv()
            value += acc_in[k, r - 1]
        out_ref[:, pl.ds(pl.multiple_of(pair_of[k] * 2 * rows, 2 * rows), 2 * rows)] = value

    for r in range(1, parts):
        sum_copy(r).wait_send()
        for k in range(pairs):
            acc_copy(k, r).wait_send()
    for flow in (1, 0):
        for s in range(last + 1):
            for c in range(chunks):
                if s == 0:
                    @pl.when(has_target(flow))
                    def _():
                        z_copy(flow, 0, c, z, own=True).wait_send()

                @pl.when(arrives(flow, s))
                def _():
                    b = arriving(flow, s)
                    for g in range(1, groups):
                        y_copy(flow, s, g, c, b, y).wait_send()
                    if s < last:
                        @pl.when(has_target(flow))
                        def _():
                            z_copy(flow, s + 1, c, b).wait_send()


def solution(mesh):
    n, groups, parts = mesh.shape["ex"], mesh.shape["groups"], mesh.shape["layer"]
    chunks = max(1, 16 // n)

    def body(queries, train_grads, layer_start):
        rows, width = queries.shape
        examples = train_grads.shape[0]
        layers = layer_start.shape[0]
        kept = examples // parts
        pairs = n // 2
        dma = pltpu.SemaphoreType.DMA
        return pl.pallas_call(
            functools.partial(kernel, n, groups, parts, chunks),
            out_shape=jax.ShapeDtypeStruct((kept, n * rows), jnp.float32),
            in_specs=[
                pl.BlockSpec(memory_space=pltpu.SMEM),
                pl.BlockSpec(memory_space=pl.ANY),
                pl.BlockSpec(memory_space=pl.ANY),
            ],
            out_specs=pl.BlockSpec(memory_space=pltpu.VMEM),
            scratch_shapes=[
                pltpu.VMEM((examples, width), jnp.bfloat16),
                pltpu.VMEM((examples, width), jnp.bfloat16),
                pltpu.VMEM((n * rows, width), jnp.bfloat16),
                pltpu.VMEM((layers, examples), jnp.float32),
                pltpu.VMEM((parts - 1, layers, examples), jnp.float32),
                pltpu.VMEM((examples, LANES), jnp.bfloat16),
                pltpu.VMEM((pairs, examples, 2 * rows), jnp.float32),
                pltpu.VMEM((pairs, parts - 1, kept, 2 * rows), jnp.float32),
                dma((chunks,)),
                dma,
                dma((2, n - 1, chunks)),
                dma((2, n - 1, chunks)),
                dma((2, n - 1, groups - 1, chunks)),
                dma((2, n - 1, groups - 1, chunks)),
                dma((parts - 1,)),
                dma((parts - 1,)),
                dma((pairs, parts - 1)),
                dma((pairs, parts - 1)),
            ],
            compiler_params=pltpu.CompilerParams(
                collective_id=0, has_side_effects=True, vmem_limit_bytes=48 * 2**20
            ),
        )(layer_start, queries, train_grads)

    return jax.shard_map(
        body,
        mesh=mesh,
        in_specs=(P("ex", "layer"), P(("groups", "ex"), "layer"), P()),
        out_specs=P(("groups", "ex", "layer"), None),
        check_vma=False,
    )
```

time: 88.7 us -> 40.3 us (0.45)
  waiting for transfers between devices: 45.4 us -> 0 us
  Pallas kernels: 0 us -> 35.9 us
  matrix products: 14.3 us -> 0 us
  blocking collectives: 13.6 us -> 0 us
  between operations: 13.4 us -> 0.01 us
  local copies, waits for them, and re-layouts: 0.92 us -> 4.23 us
    pallas_call x0 -> x1, Pallas kernels: none -> 35.9 us  [body(): pl.pallas_call(functools.partial(kernel, n, groups, parts, chunks), out_s...]
    all_gather x1 -> x0, waiting for transfers between devices: 25 us -> none  [body(): every_q = lax.all_gather(queries, 'ex', axis=0, tiled=True)]
    reduce_scatter x1 -> x0, waiting for transfers between devices: 19.7 us -> none  [body(): lax.psum_scatter(partial_value, 'layer', scatter_dimension=0, tiled=True)]
    dot_general x3 -> x0, matrix products: 14.3 us -> none  [the longest x1 5.42 us: body(): jnp.dot(widened * widened, member, precision=lax.Precision.HIGHEST)]
    psum x1 -> x0, blocking collectives: 13.6 us -> none  [body(): square_sums = lax.psum(local_sums, 'layer')]
    unnamed x4 -> x7, local copies, waits for them, and re-layouts: 0.01 us -> 4.23 us
    slice x1 -> x0, local copies, waits for them, and re-layouts: 0.91 us -> none  [body(): layer_start[1:]]
  transfers between devices with their start and end apart: 2 -> 0, of which waited for: 2 -> 0; matrix products, arithmetic and copies ran while one was open for 13% -> 0% of each run, Pallas kernels for 0% -> 0%
where the time goes in v1:
time: 40.3 us; the launch traced here: 40.1 us
  Pallas kernels  35.9 us (89%)
  local copies, waits for them, and re-layouts  4.23 us (10%)
    pallas_call x1, Pallas kernels, body(): pl.pallas_call(functools.partial(kernel, n, groups, parts, chunks), out_s...  35.9 us
    unnamed x7, local copies, waits for them, and re-layouts  4.23 us

profile of v1, /device:TPU:0, one launch (start us, length us, event | category | flops | bytes accessed | tf_op | source)
XLA Modules:
  0.0 40.1 jit_solution(728461483649117102)
XLA Ops:
  0.0 0.0 copy-start
  0.0 1.9 %copy-done = bf16[384,4096]{1,0:T(8,128)(2,1)S(1)} copy-done((bf16[384,4096]{1,0:T(8,128)(2,1)S(1)}, bf16[384,4096]{1,0:T(8,128)(2,1)}, u32[]{:S(2)}) %copy-start) | copy-done | bytes 3145752
  1.9 0.0 copy-start.1
  1.9 1.0 %copy-done.1 = bf16[64,4096]{1,0:T(8,128)(2,1)S(1)} copy-done((bf16[64,4096]{1,0:T(8,128)(2,1)S(1)}, bf16[64,4096]{1,0:T(8,128)(2,1)}, u32[]{:S(2)}) %copy-start.1) | copy-done | bytes 524312
  2.9 0.0 copy-start.2
  2.9 0.7 %copy-done.2 = s32[32]{0:T(128)S(1)} copy-done((s32[32]{0:T(128)S(1)}, s32[32]{0:T(128)}, u32[]{:S(2)}) %copy-start.2) | copy-done | bytes 152
  3.6 35.9 %shard_map.37 = f32[96,256]{1,0:T(8,128)S(1)} custom-call(s32[32]{0:T(128)S(1)} %copy-done.2, bf16[64,4096]{1,0:T(8,128)(2,1)S(1)} %copy-done.1, bf16[384,4096]{1,0:T(8,128)(2,1)S(1)} %copy-done), custom_call_target="tpu_custom_call" | custom-call | tf_op jit(solution)/shard_map/pallas_call | solution.py:272
  39.5 0.6 %copy.5 = f32[96,256]{1,0:T(8,128)} copy(f32[96,256]{1,0:T(8,128)S(1)} %shard_map.37) | data formatting | bytes 196608
Async XLA Ops:
  0.0 1.9 %copy-start = (bf16[384,4096]{1,0:T(8,128)(2,1)S(1)}, bf16[384,4096]{1,0:T(8,128)(2,1)}, u32[]{:S(2)}) copy-start(bf16[384,4096]{1,0:T(8,128)(2,1)} %x_hbm.1) | copy-start | bytes 9437188
  1.9 1.0 %copy-start.1 = (bf16[64,4096]{1,0:T(8,128)(2,1)S(1)}, bf16[64,4096]{1,0:T(8,128)(2,1)}, u32[]{:S(2)}) copy-start(bf16[64,4096]{1,0:T(8,128)(2,1)} %q_ref.1) | copy-start | bytes 1572868
  2.9 0.7 %copy-start.2 = (s32[32]{0:T(128)S(1)}, s32[32]{0:T(128)}, u32[]{:S(2)}) copy-start(s32[32]{0:T(128)} %start_ref.1) | copy-start | bytes 388

commit v2 on v1

--- a/solution.py
+++ b/solution.py
@@ -18,9 +18,9 @@
 
 
 def kernel(
-    n, groups, parts, chunks, start_ref, q_ref, x_hbm, out_ref,
-    x_v, scaled_v, q_all, sums, sums_in, inv_v, acc, acc_in,
-    x_sem, q_sem, z_send, z_recv, y_send, y_recv, sum_send, sum_recv, acc_send, acc_recv,
+    n, groups, parts, chunks, swapped, start_hbm, q_ref, x_hbm, out_ref,
+    start_ref, x_v, scaled_v, q_all, sums, sums_in, inv_v, acc, acc_in,
+    start_sem, x_sem, q_sem, z_send, z_recv, y_send, y_recv, sum_send, sum_recv, acc_send, acc_recv,
 ):
     y, z, me = lax.axis_index("groups"), lax.axis_index("ex"), lax.axis_index("layer")
     rows, width = q_ref.shape
@@ -28,7 +28,7 @@
     chunk = width // chunks
     examples = x_hbm.shape[0]
     kept = examples // parts
-    layers = start_ref.shape[0]
+    layers = start_hbm.shape[0]
     last = n - 2
     pairs = n // 2
 
@@ -41,6 +41,9 @@
     def block_rows(b):
         return pl.ds(pl.multiple_of(b * rows, rows), rows)
 
+    def q_copy(c):
+        return pltpu.make_async_copy(q_ref.at[:, cols(c)], q_all.at[c, block_rows(z)], q_sem.at[c])
+
     def share_rows(b, g):
         return pl.ds(pl.multiple_of(b * rows + g * share, share), share)
 
@@ -56,17 +59,30 @@
     def arrives(flow, s):
         return z - 1 - s >= 0 if flow == 0 else z + 1 + s < n
 
-    def z_copy(flow, s, c, b, own=False):
-        there = q_all.at[share_rows(b, y), cols(c)]
-        here = q_ref.at[pl.ds(pl.multiple_of(y * share, share), share), cols(c)] if own else there
+    def is_edge(flow, b):
+        return b == (0 if flow == 0 else n - 1)
+
+    def by_kind(flow, b, c, act):
+        if c < swapped:
+            act(False)
+        else:
+            edge = is_edge(flow, b)
+            pl.when(edge)(lambda: act(True))
+            pl.when(jnp.logical_not(edge))(lambda: act(False))
+
+    def z_copy(flow, s, c, b, whole, own=False):
+        there = q_all.at[c, block_rows(b) if whole else share_rows(b, y)]
+        here = there
+        if own:
+            here = q_ref.at[:, cols(c)] if whole else q_ref.at[pl.ds(pl.multiple_of(y * share, share), share), cols(c)]
         return pltpu.make_async_remote_copy(
-            src_ref=here, dst_ref=there, send_sem=z_send.at[flow, s, c], recv_sem=z_recv.at[flow, s, c],
+            src_ref=here, dst_ref=there, send_sem=z_send.at[flow, s], recv_sem=z_recv.at[flow, s, c],
             device_id={"ex": z_target(flow)}, device_id_type=MESH)
 
     def y_copy(flow, s, g, c, b, owner):
-        block = q_all.at[share_rows(b, owner), cols(c)]
+        block = q_all.at[c, share_rows(b, owner)]
         return pltpu.make_async_remote_copy(
-            src_ref=block, dst_ref=block, send_sem=y_send.at[flow, s, g - 1, c], recv_sem=y_recv.at[flow, s, g - 1, c],
+            src_ref=block, dst_ref=block, send_sem=y_send.at[flow, s, g - 1], recv_sem=y_recv.at[flow, s, g - 1, c],
             device_id={"groups": lax.rem(y + g, groups)}, device_id_type=MESH)
 
     def sum_copy(r):
@@ -81,31 +97,64 @@
             send_sem=acc_send.at[k, r - 1], recv_sem=acc_recv.at[k, r - 1],
             device_id={"layer": to}, device_id_type=MESH)
 
+    def z_sends(flow, s):
+        return has_target(flow) if s == 0 else has_target(flow) & arrives(flow, s - 1)
+
+    def wait_sends(s):
+        def wait(due, semaphore, count):
+            if count:
+                @pl.when(due)
+                def _():
+                    lead = pl.cdiv(count, n * rows)
+                    sent = q_all.at[pl.ds(0, lead), pl.ds(0, count // lead)]
+                    pltpu.make_async_copy(sent, sent, semaphore).wait()
+
+        full, less, more = chunks * share, swapped * share, swapped * share + (chunks - swapped) * rows
+        for flow in (1, 0):
+            edge = is_edge(flow, z if s == 0 else arriving(flow, s - 1))
+            wait(z_sends(flow, s) & edge, z_send.at[flow, s], more)
+            wait(z_sends(flow, s) & jnp.logical_not(edge), z_send.at[flow, s], full)
+            edge = is_edge(flow, arriving(flow, s))
+            for g in range(1, groups):
+                wait(arrives(flow, s) & edge, y_send.at[flow, s, g - 1], less)
+                wait(arrives(flow, s) & jnp.logical_not(edge), y_send.at[flow, s, g - 1], full)
+
     def handle(s, c):
         for flow in (1, 0):
-            @pl.when(arrives(flow, s))
-            def _():
-                b = arriving(flow, s)
-                z_copy(flow, s, c, b).wait_recv()
-                for g in range(1, groups):
-                    y_copy(flow, s, g, c, b, y).start()
+            b = arriving(flow, s)
+
+            def act(whole):
+                z_copy(flow, s, c, b, whole).wait_recv()
+                if not whole:
+                    for g in range(1, groups):
+                        y_copy(flow, s, g, c, b, y).start()
                 if s < last:
                     @pl.when(has_target(flow))
                     def _():
-                        z_copy(flow, s + 1, c, b).start()
+                        z_copy(flow, s + 1, c, b, whole).start()
+
+            @pl.when(arrives(flow, s))
+            def _():
+                by_kind(flow, b, c, act)
 
     def wait_y(s, c):
         for flow in (1, 0):
-            @pl.when(arrives(flow, s))
+            b = arriving(flow, s)
+            due = arrives(flow, s)
+            if c >= swapped:
+                due = due & jnp.logical_not(is_edge(flow, b))
+
+            @pl.when(due)
             def _():
-                b = arriving(flow, s)
                 for g in range(1, groups):
                     y_copy(flow, s, g, c, b, lax.rem(y + groups - g, groups)).wait_recv()
 
+    start_copy = pltpu.make_async_copy(start_hbm, start_ref, start_sem)
+    start_copy.start()
     for c in range(chunks):
         x_copy(c).start()
-    q_copy = pltpu.make_async_copy(q_ref, q_all.at[block_rows(z)], q_sem)
-    q_copy.start()
+    for c in range(chunks):
+        q_copy(c).start()
 
     barrier = pltpu.get_barrier_semaphore()
     for flow in (0, 1):
@@ -123,8 +172,9 @@
         for flow in (1, 0):
             @pl.when(has_target(flow))
             def _():
-                z_copy(flow, 0, c, z, own=True).start()
-
+                by_kind(flow, z, c, lambda whole: z_copy(flow, 0, c, z, whole, own=True).start())
+
+    start_copy.wait()
     starts = [start_ref[l] for l in range(layers)]
     ends = starts[1:] + [WIDTH]
     offset = me * width
@@ -158,12 +208,13 @@
     for r in range(1, parts):
         sum_copy(r).start()
 
-    q_copy.wait()
+    for c in range(chunks):
+        q_copy(c).wait()
     own_pair = z // 2
 
     def pair_dot(k, p, c):
         pair = pl.ds(pl.multiple_of(p * 2 * rows, 2 * rows), 2 * rows)
-        value = nt_dot(scaled_v[:, cols(c)], q_all[pair, cols(c)])
+        value = nt_dot(scaled_v[:, cols(c)], q_all[c, pair])
         if c == 0:
             acc[k] = value
         else:
@@ -208,7 +259,8 @@
     for s in range(2, last):
         for c in range(chunks):
             handle(s, c)
-    handle(last, 0)
+    for c in range(swapped):
+        handle(last, c)
     for s in range(1, last):
         for c in range(chunks):
             wait_y(s, c)
@@ -221,12 +273,17 @@
         send_pair(k)
     pair_of.append(last_pair)
     for c in range(chunks):
-        if c + 1 < chunks:
-            handle(last, c + 1)
-        wait_y(last, c)
+        if c < swapped:
+            wait_y(last, c)
+        else:
+            handle(last, c)
         pair_dot(pairs - 1, last_pair, c)
     send_pair(pairs - 1)
 
+    for s in range(last + 1):
+        wait_sends(s)
+    for r in range(1, parts):
+        sum_copy(r).wait_send()
     mine = pl.ds(pl.multiple_of(me * kept, 8), kept)
     for k in range(pairs):
         value = acc[k, mine]
@@ -234,33 +291,15 @@
             acc_copy(k, r).wait_recv()
             value += acc_in[k, r - 1]
         out_ref[:, pl.ds(pl.multiple_of(pair_of[k] * 2 * rows, 2 * rows), 2 * rows)] = value
-
-    for r in range(1, parts):
-        sum_copy(r).wait_send()
-        for k in range(pairs):
+    for k in range(pairs):
+        for r in range(1, parts):
             acc_copy(k, r).wait_send()
-    for flow in (1, 0):
-        for s in range(last + 1):
-            for c in range(chunks):
-                if s == 0:
-                    @pl.when(has_target(flow))
-                    def _():
-                        z_copy(flow, 0, c, z, own=True).wait_send()
-
-                @pl.when(arrives(flow, s))
-                def _():
-                    b = arriving(flow, s)
-                    for g in range(1, groups):
-                        y_copy(flow, s, g, c, b, y).wait_send()
-                    if s < last:
-                        @pl.when(has_target(flow))
-                        def _():
-                            z_copy(flow, s + 1, c, b).wait_send()
 
 
 def solution(mesh):
     n, groups, parts = mesh.shape["ex"], mesh.shape["groups"], mesh.shape["layer"]
     chunks = max(1, 16 // n)
+    swapped = chunks - chunks // 2
 
     def body(queries, train_grads, layer_start):
         rows, width = queries.shape
@@ -270,28 +309,30 @@
         pairs = n // 2
         dma = pltpu.SemaphoreType.DMA
         return pl.pallas_call(
-            functools.partial(kernel, n, groups, parts, chunks),
+            functools.partial(kernel, n, groups, parts, chunks, swapped),
             out_shape=jax.ShapeDtypeStruct((kept, n * rows), jnp.float32),
             in_specs=[
-                pl.BlockSpec(memory_space=pltpu.SMEM),
-                pl.BlockSpec(memory_space=pl.ANY),
-                pl.BlockSpec(memory_space=pl.ANY),
+                pl.BlockSpec(memory_space=pltpu.HBM),
+                pl.BlockSpec(memory_space=pltpu.HBM),
+                pl.BlockSpec(memory_space=pltpu.HBM),
             ],
             out_specs=pl.BlockSpec(memory_space=pltpu.VMEM),
             scratch_shapes=[
+                pltpu.SMEM((layers,), jnp.int32),
                 pltpu.VMEM((examples, width), jnp.bfloat16),
                 pltpu.VMEM((examples, width), jnp.bfloat16),
-                pltpu.VMEM((n * rows, width), jnp.bfloat16),
+                pltpu.VMEM((chunks, n * rows, width // chunks), jnp.bfloat16),
                 pltpu.VMEM((layers, examples), jnp.float32),
                 pltpu.VMEM((parts - 1, layers, examples), jnp.float32),
                 pltpu.VMEM((examples, LANES), jnp.bfloat16),
                 pltpu.VMEM((pairs, examples, 2 * rows), jnp.float32),
                 pltpu.VMEM((pairs, parts - 1, kept, 2 * rows), jnp.float32),
+                dma,
                 dma((chunks,)),
-                dma,
+                dma((chunks,)),
+                dma((2, n - 1)),
                 dma((2, n - 1, chunks)),
-                dma((2, n - 1, chunks)),
-                dma((2, n - 1, groups - 1, chunks)),
+                dma((2, n - 1, groups - 1)),
                 dma((2, n - 1, groups - 1, chunks)),
                 dma((parts - 1,)),
                 dma((parts - 1,)),
@@ -299,7 +340,7 @@
                 dma((pairs, parts - 1)),
             ],
             compiler_params=pltpu.CompilerParams(
-                collective_id=0, has_side_effects=True, vmem_limit_bytes=48 * 2**20
+                collective_id=0, has_side_effects=True, vmem_limit_bytes=60 * 2**20
             ),
         )(layer_start, queries, train_grads)
 

time: 40.3 us -> 34.5 us (0.86)
  Pallas kernels: 35.9 us -> 32.8 us
  local copies, waits for them, and re-layouts: 4.23 us -> 1.54 us
    pallas_call x1, Pallas kernels: 35.9 us -> 32.8 us  [body(): pl.pallas_call(functools.partial(kernel, n, groups, parts, chunks, swappe...]
    unnamed x7 -> x1, local copies, waits for them, and re-layouts: 4.23 us -> 1.54 us
where the time goes in v2:
time: 34.5 us; the launch traced here: 34.4 us
  Pallas kernels  32.8 us (95%)
  local copies, waits for them, and re-layouts  1.54 us (4%)
    pallas_call x1, Pallas kernels, body(): pl.pallas_call(functools.partial(kernel, n, groups, parts, chunks, swappe...  32.8 us
    unnamed x1, local copies, waits for them, and re-layouts  1.54 us

profile of v2, /device:TPU:0, one launch (start us, length us, event | category | flops | bytes accessed | tf_op | source)
XLA Modules:
  0.0 34.4 jit_solution(16633056332423796548)
XLA Ops:
  0.0 32.8 %shard_map.37 = f32[96,256]{1,0:T(8,128)} custom-call(s32[32]{0:T(128)} %start_hbm.1, bf16[64,4096]{1,0:T(8,128)(2,1)} %q_ref.1, bf16[384,4096]{1,0:T(8,128)(2,1)} %x_hbm.1), custom_call_target="tpu_custom_call" | custom-call | tf_op jit(solution)/shard_map/pallas_call | solution.py:311
  32.8 1.5 %copy.5 = f32[96,256]{1,0:T(8,128)} copy(f32[96,256]{1,0:T(8,128)} %shard_map.37) | data formatting | bytes 196608

commit v3 on v2

--- a/solution.py
+++ b/solution.py
@@ -19,8 +19,8 @@
 
 def kernel(
     n, groups, parts, chunks, swapped, start_hbm, q_ref, x_hbm, out_ref,
-    start_ref, x_v, scaled_v, q_all, sums, sums_in, inv_v, acc, acc_in,
-    start_sem, x_sem, q_sem, z_send, z_recv, y_send, y_recv, sum_send, sum_recv, acc_send, acc_recv,
+    start_ref, x_v, scaled_v, q_all, sums, sums_in, inv_v, acc, acc_in, half, half_out, half_in,
+    start_sem, x_sem, q_sem, z_send, z_recv, y_send, y_recv, sum_send, sum_recv, acc_send, acc_recv, half_send, half_recv,
 ):
     y, z, me = lax.axis_index("groups"), lax.axis_index("ex"), lax.axis_index("layer")
     rows, width = q_ref.shape
@@ -118,6 +118,35 @@
             for g in range(1, groups):
                 wait(arrives(flow, s) & edge, y_send.at[flow, s, g - 1], less)
                 wait(arrives(flow, s) & jnp.logical_not(edge), y_send.at[flow, s, g - 1], full)
+
+    def half_copy(i, r):
+        return pltpu.make_async_remote_copy(
+            src_ref=half_out.at[i, r - 1], dst_ref=half_in.at[i, r - 1],
+            send_sem=half_send.at[i, r - 1], recv_sem=half_recv.at[i, r - 1],
+            device_id={"layer": lax.rem(me + r, parts)}, device_id_type=MESH)
+
+    def packed(i, to):
+        value = half[i, pl.ds(pl.multiple_of(to * kept, 8), kept)]
+        return jnp.concatenate([value[:kept // 2], value[kept // 2:]], axis=1)
+
+    def send_half(i):
+        for r in range(1, parts):
+            half_out[i, r - 1] = packed(i, lax.rem(me + r, parts))
+            half_copy(i, r).start()
+
+    def half_dot(i, b, c):
+        value = nt_dot(scaled_v[:, cols(c)], q_all[c, block_rows(b)])
+        if c == 0:
+            half[i] = value
+        else:
+            half[i] += value
+
+    def half_total(i):
+        value = packed(i, me)
+        for r in range(1, parts):
+            half_copy(i, r).wait_recv()
+            value += half_in[i, r - 1]
+        return jnp.concatenate([value[:, :rows], value[:, rows:]], axis=0)
 
     def handle(s, c):
         for flow in (1, 0):
@@ -168,11 +197,15 @@
     peers = groups + parts - jnp.where(z == 0, 1, 0) - jnp.where(z == n - 1, 1, 0)
     pl.semaphore_wait(barrier, peers)
 
-    for c in range(chunks):
+    def send_own(c):
         for flow in (1, 0):
             @pl.when(has_target(flow))
             def _():
                 by_kind(flow, z, c, lambda whole: z_copy(flow, 0, c, z, whole, own=True).start())
+
+    ahead_sends = 2
+    for c in range(min(ahead_sends, chunks)):
+        send_own(c)
 
     start_copy.wait()
     starts = [start_ref[l] for l in range(layers)]
@@ -203,7 +236,11 @@
         small = (square - big.astype(jnp.float32)).astype(jnp.bfloat16)
         total += jnp.dot(big, member, preferred_element_type=jnp.float32)
         total += jnp.dot(small, member, preferred_element_type=jnp.float32)
-        handle(0, c)
+        if c + ahead_sends < chunks:
+            send_own(c + ahead_sends)
+        if c:
+            handle(0, c - 1)
+    handle(0, chunks - 1)
     sums[...] = total.T[:layers]
     for r in range(1, parts):
         sum_copy(r).start()
@@ -271,29 +308,39 @@
         for c in range(chunks):
             pair_dot(k, p, c)
         send_pair(k)
-    pair_of.append(last_pair)
+    near, far = jnp.where(ahead, n - 2, 1), jnp.where(ahead, n - 1, 0)
+    for c in range(chunks):
+        half_dot(0, near, c)
+    send_half(0)
     for c in range(chunks):
         if c < swapped:
             wait_y(last, c)
         else:
             handle(last, c)
-        pair_dot(pairs - 1, last_pair, c)
-    send_pair(pairs - 1)
+        half_dot(1, far, c)
+    send_half(1)
 
     for s in range(last + 1):
         wait_sends(s)
     for r in range(1, parts):
         sum_copy(r).wait_send()
     mine = pl.ds(pl.multiple_of(me * kept, 8), kept)
-    for k in range(pairs):
+    for k in range(pairs - 1):
         value = acc[k, mine]
         for r in range(1, parts):
             acc_copy(k, r).wait_recv()
             value += acc_in[k, r - 1]
         out_ref[:, pl.ds(pl.multiple_of(pair_of[k] * 2 * rows, 2 * rows), 2 * rows)] = value
-    for k in range(pairs):
-        for r in range(1, parts):
+    for r in range(1, parts):
+        for k in range(pairs - 1):
             acc_copy(k, r).wait_send()
+        half_copy(0, r).wait_send()
+    near_total = half_total(0)
+    far_total = half_total(1)
+    first, second = jnp.where(ahead, near_total, far_total), jnp.where(ahead, far_total, near_total)
+    out_ref[:, pl.ds(pl.multiple_of(last_pair * 2 * rows, 2 * rows), 2 * rows)] = jnp.concatenate([first, second], axis=1)
+    for r in range(1, parts):
+        half_copy(1, r).wait_send()
 
 
 def solution(mesh):
@@ -325,8 +372,11 @@
                 pltpu.VMEM((layers, examples), jnp.float32),
                 pltpu.VMEM((parts - 1, layers, examples), jnp.float32),
                 pltpu.VMEM((examples, LANES), jnp.bfloat16),
-                pltpu.VMEM((pairs, examples, 2 * rows), jnp.float32),
-                pltpu.VMEM((pairs, parts - 1, kept, 2 * rows), jnp.float32),
+                pltpu.VMEM((pairs - 1, examples, 2 * rows), jnp.float32),
+                pltpu.VMEM((pairs - 1, parts - 1, kept, 2 * rows), jnp.float32),
+                pltpu.VMEM((2, examples, rows), jnp.float32),
+                pltpu.VMEM((2, parts - 1, kept // 2, 2 * rows), jnp.float32),
+                pltpu.VMEM((2, parts - 1, kept // 2, 2 * rows), jnp.float32),
                 dma,
                 dma((chunks,)),
                 dma((chunks,)),
@@ -336,8 +386,10 @@
                 dma((2, n - 1, groups - 1, chunks)),
                 dma((parts - 1,)),
                 dma((parts - 1,)),
-                dma((pairs, parts - 1)),
-                dma((pairs, parts - 1)),
+                dma((pairs - 1, parts - 1)),
+                dma((pairs - 1, parts - 1)),
+                dma((2, parts - 1)),
+                dma((2, parts - 1)),
             ],
             compiler_params=pltpu.CompilerParams(
                 collective_id=0, has_side_effects=True, vmem_limit_bytes=60 * 2**20

time: 34.5 us -> 34 us (0.986)
  Pallas kernels: 32.8 us -> 32.4 us
    pallas_call x1, Pallas kernels: 32.8 us -> 32.4 us  [body(): pl.pallas_call(functools.partial(kernel, n, groups, parts, chunks, swappe...]
where the time goes in v3:
time: 34 us; the launch traced here: 33.9 us
  Pallas kernels  32.4 us (95%)
  local copies, waits for them, and re-layouts  1.54 us (5%)
    pallas_call x1, Pallas kernels, body(): pl.pallas_call(functools.partial(kernel, n, groups, parts, chunks, swappe...  32.4 us
    unnamed x1, local copies, waits for them, and re-layouts  1.54 us

profile of v3, /device:TPU:0, one launch (start us, length us, event | category | flops | bytes accessed | tf_op | source)
XLA Modules:
  0.0 33.9 jit_solution(6328505983957458868)
XLA Ops:
  0.0 32.4 %shard_map.37 = f32[96,256]{1,0:T(8,128)} custom-call(s32[32]{0:T(128)} %start_hbm.1, bf16[64,4096]{1,0:T(8,128)(2,1)} %q_ref.1, bf16[384,4096]{1,0:T(8,128)(2,1)} %x_hbm.1), custom_call_target="tpu_custom_call" | custom-call | tf_op jit(solution)/shard_map/pallas_call | solution.py:358
  32.4 1.5 %copy.5 = f32[96,256]{1,0:T(8,128)} copy(f32[96,256]{1,0:T(8,128)} %shard_map.37) | data formatting | bytes 196608
